TPU v7x, 32 devices: a whole 2x2x4 slice. The times are simulated.
32 devices in a mesh: tex: 4 (over x, core), smp: 8 (over z, y).
Axes of the slice: x: 2, y: 2, z: 4, core: 2. Of those that a mesh axis runs over, the one named last changes fastest.
Arguments:
- blocks: int32 [4, 8, 2, 2], P('tex', 'smp'), may hold values from -1 to 3, as said below
- observed: float32 [4, 8, 512, 256], P('tex', 'smp'), may hold values from 0.05 to 1.5
- w_factor: float32 [64, 4096], P('smp', 'tex'), may hold values from 0.03 to 0.5
- h_factor: float32 [64, 8192], P('tex', 'smp'), may hold values from 0.03 to 0.5
Outputs:
- w_final: float32 [64, 4096], P('smp', 'tex')
- h_final: float32 [64, 8192], P('tex', 'smp')
Inputs may be any that keep to these rules, and one draw needn't show every extreme that they name: blocks[t, s, 0, j] is a block row (below 4) and blocks[t, s, 1, j] a block column (below 4) of device (t, s)'s tile, or both are -1 for an empty slot; live slots come first and name different blocks; each device has at least one live slot and some device has 2; every block row of texels is observed on some device along smp, and every block column of samples on some device along tex.
All inputs are finite; a program needn't handle non-finite values.
Results may differ from a plain program's by a relative error of at most 0.0003.
Values sent between devices are 32-bit elements; how exact they have to be, the bound alone decides.
A program may use at most 64 MiB of HBM per device.

v0:
```python
import jax
import jax.numpy as jnp
from jax import lax
from jax.sharding import PartitionSpec as P

BS = 256
RB = 4
CB = 4
CAP = 2
ITERS = 2


highest = lax.Precision.HIGHEST


def pick_tables(listing, rows_count, cols_count):
    rows = listing[0]
    cols = listing[1]
    live = (rows >= 0).astype(jnp.float32)
    row_pick = (jnp.maximum(rows, 0)[:, None] == jnp.arange(rows_count)[None, :]).astype(
        jnp.float32
    ) * live[:, None]
    col_pick = (jnp.maximum(cols, 0)[:, None] == jnp.arange(cols_count)[None, :]).astype(
        jnp.float32
    )
    return (row_pick, col_pick)


def block_factors(w_tile, h_tile, row_pick, col_pick):
    rank = w_tile.shape[0]
    w_blocks = jnp.einsum(
        "sr,krb->skb", row_pick, w_tile.reshape(rank, row_pick.shape[1], -1), precision=highest
    )
    h_blocks = jnp.einsum(
        "sc,kcb->skb", col_pick, h_tile.reshape(rank, col_pick.shape[1], -1), precision=highest
    )
    approx = jnp.einsum("ska,skb->sab", w_blocks, h_blocks, precision=highest)
    return (w_blocks, h_blocks, approx)


def basis_terms(w_tile, h_tile, row_pick, col_pick, values):
    w_blocks, h_blocks, approx = block_factors(w_tile, h_tile, row_pick, col_pick)
    upper = jnp.einsum("ska,sab->skb", w_blocks, values, precision=highest)
    lower = jnp.einsum("ska,sab->skb", w_blocks, approx, precision=highest)
    upper = jnp.einsum("sc,skb->kcb", col_pick, upper, precision=highest)
    lower = jnp.einsum("sc,skb->kcb", col_pick, lower, precision=highest)
    return (upper.reshape(h_tile.shape), lower.reshape(h_tile.shape))


def weight_terms(w_tile, h_tile, row_pick, col_pick, values):
    w_blocks, h_blocks, approx = block_factors(w_tile, h_tile, row_pick, col_pick)
    upper = jnp.einsum("skb,sab->ska", h_blocks, values, precision=highest)
    lower = jnp.einsum("skb,sab->ska", h_blocks, approx, precision=highest)
    upper = jnp.einsum("sr,ska->kra", row_pick, upper, precision=highest)
    lower = jnp.einsum("sr,ska->kra", row_pick, lower, precision=highest)
    return (upper.reshape(w_tile.shape), lower.reshape(w_tile.shape))


def per_device(blocks, observed, w_factor, h_factor):
    row_pick, col_pick = pick_tables(blocks[0, 0], RB, CB)
    values = observed[0, 0].reshape(CAP, BS, BS)
    w_full = lax.all_gather(w_factor, "smp", axis=0, tiled=True)
    h_full = lax.all_gather(h_factor, "tex", axis=0, tiled=True)
    for sweep in range(ITERS):
        upper, lower = basis_terms(w_full, h_full, row_pick, col_pick, values)
        upper, lower = lax.psum((upper, lower), "tex")
        h_full = h_full * upper / lower
        upper, lower = weight_terms(w_full, h_full, row_pick, col_pick, values)
        upper, lower = lax.psum((upper, lower), "smp")
        w_full = w_full * upper / lower
    h_rows = h_factor.shape[0]
    w_rows = w_factor.shape[0]
    h_share = lax.dynamic_slice_in_dim(h_full, lax.axis_index("tex") * h_rows, h_rows, 0)
    w_share = lax.dynamic_slice_in_dim(w_full, lax.axis_index("smp") * w_rows, w_rows, 0)
    return (w_share, h_share)


def solution(mesh):
    in_specs = (
        P("tex", "smp", None, None),
        P("tex", "smp", None, None),
        P("smp", "tex"),
        P("tex", "smp"),
    )
    out_specs = (P("smp", "tex"), P("tex", "smp"))
    return jax.shard_map(
        per_device, mesh=mesh, in_specs=in_specs, out_specs=out_specs, check_vma=False
    )
```

profile of v0, /device:TPU:0, one launch (start us, length us, event | category | flops | bytes accessed | tf_op | source)
XLA Modules:
  0.0 291.8 jit_solution(4560743736998129889)
XLA Ops:
  7.2 0.7 maximum_bitcast_fusion
  8.0 32.7 %all_gather.6 = f32[64,1024]{1,0:T(8,128)S(1)} all-gather(f32[8,1024]{1,0:T(8,128)} %param.6), channel_id=1, replica_groups=mesh['tex'=4,'smp'=8] {'smp'}, dimensions={0}, use_global_device_ids=true | all-gather | bytes 294912 | tf_op jit(solution)/shard_map/all_gather | solution.py:62
  40.9 0.7 copy-done.1
  41.6 5.8 %all_gather.7 = f32[64,1024]{1,0:T(8,128)S(1)} all-gather(f32[16,1024]{1,0:T(8,128)S(1)} %copy-done.1), channel_id=1, replica_groups=mesh['tex'=4,'smp'=8] {'tex'}, dimensions={0}, use_global_device_ids=true | all-gather | bytes 327680 | tf_op jit(solution)/shard_map/all_gather | solution.py:63
  47.5 0.4 fusion.51
  47.9 0.6 fusion.69
  48.5 0.6 fusion.14
  49.2 0.4 fusion.39
  49.6 0.5 fusion.12
  50.1 0.7 copy.20
  50.8 0.4 fusion.42
  51.3 0.5 fusion.16
  51.8 0.8 copy.19
  52.6 34.4 %all-reduce.15.cloned.1.call-done = (f32[64,1024]{1,0:T(8,128)}, f32[64,1024]{1,0:T(8,128)}) async-done(((f32[64,1024]{1,0:T(8,128)}, f32[64,1024]{1,0:T(8,128)}), (f32[64,1024]{1,0:T(8,128)}, f32[64,1024]{1,0:T(8,128)})) %all-reduce.15.cloned.1.call-update) | async-done | bytes 524304 | tf_op jit(solution)/shard_map/psum | solution.py:66
  87.0 1.1 multiply_divide_fusion.2
  88.1 0.1 reshape.78
  88.2 0.4 fusion.48
  88.6 0.6 fusion.34
  89.3 0.6 fusion.36
  89.9 0.6 fusion.32
  90.5 0.7 fusion.8
  91.2 0.7 copy.22
  91.9 0.7 fusion.10
  92.6 0.8 copy.21
  93.4 72.8 %all-reduce.11.cloned.1.call-done = (f32[64,1024]{1,0:T(8,128)}, f32[64,1024]{1,0:T(8,128)}) async-done(((f32[64,1024]{1,0:T(8,128)}, f32[64,1024]{1,0:T(8,128)}), (f32[64,1024]{1,0:T(8,128)}, f32[64,1024]{1,0:T(8,128)})) %all-reduce.11.cloned.1.call-update) | async-done | bytes 524304 | tf_op jit(solution)/shard_map/psum | solution.py:69
  166.2 1.1 multiply_divide_fusion.1
  167.4 0.6 fusion.65
  168.1 0.6 fusion.27
  168.7 0.4 fusion.29
  169.1 0.4 fusion.25
  169.6 0.5 fusion.4
  170.1 0.7 copy.24
  170.8 0.5 fusion.6
  171.3 0.8 copy.23
  172.1 0.2 all-reduce.9.cloned.1.call-start
  172.3 32.3 %all-reduce.13.cloned.1.call-done = (f32[64,1024]{1,0:T(8,128)}, f32[64,1024]{1,0:T(8,128)}) async-done(((f32[64,1024]{1,0:T(8,128)}, f32[64,1024]{1,0:T(8,128)}), (f32[64,1024]{1,0:T(8,128)}, f32[64,1024]{1,0:T(8,128)})) %all-reduce.13.cloned.1.call-update) | async-done | bytes 524304 | tf_op jit(solution)/shard_map/psum | solution.py:66
  204.6 1.1 multiply_divide_fusion
  205.9 0.4 fusion.44
  206.3 0.6 fusion.20
  206.9 0.6 fusion.22
  207.5 0.6 fusion.18
  208.1 0.7 fusion
  208.8 0.7 copy.26
  209.5 0.7 fusion.2
  210.2 0.8 copy.25
  211.0 0.6 constant_dynamic-slice_fusion
  211.7 72.2 %all-reduce.9.cloned.1.call-done = (f32[64,1024]{1,0:T(8,128)}, f32[64,1024]{1,0:T(8,128)}) async-done(((f32[64,1024]{1,0:T(8,128)}, f32[64,1024]{1,0:T(8,128)}), (f32[64,1024]{1,0:T(8,128)}, f32[64,1024]{1,0:T(8,128)})) %all-reduce.9.cloned.1.call-update) | async-done | bytes 524304 | tf_op jit(solution)/shard_map/psum | solution.py:69
  283.9 1.4 dynamic-slice_divide_fusion
  (17 shorter events, 0.7 us)
Async XLA Ops:
  7.2 43.7 %copy-start = (f32[1,1,512,256]{3,2,1,0:T(8,128)S(1)}, f32[1,1,512,256]{3,2,1,0:T(8,128)}, u32[]{:S(2)}) copy-start(f32[1,1,512,256]{3,2,1,0:T(8,128)} %param.5) | copy-start | bytes 1572868
  7.2 0.8 copy-start.2
  7.2 79.8 %all-reduce.15.cloned.1.call-start = ((), (), s32[]{:S(2)}) async-start(), calls=%async_computation.3 | async-start | bytes 1048576 | tf_op jit(solution)/shard_map/psum | solution.py:66
  40.7 0.8 copy-start.1
  52.6 113.6 %all-reduce.11.cloned.1.call-start = ((), (), s32[]{:S(2)}) async-start(), calls=%async_computation.1 | async-start | bytes 1048576 | tf_op jit(solution)/shard_map/psum | solution.py:69
  93.4 111.3 %all-reduce.13.cloned.1.call-start = ((), (), s32[]{:S(2)}) async-start(), calls=%async_computation.2 | async-start | bytes 1048576 | tf_op jit(solution)/shard_map/psum | solution.py:66
  172.1 111.8 %all-reduce.9.cloned.1.call-start = ((), (), s32[]{:S(2)}) async-start(), calls=%async_computation | async-start | bytes 1048576 | tf_op jit(solution)/shard_map/psum | solution.py:69
Sparse Core Ops, SparseCore 0:
  52.7 34.2 all-reduce.14
  93.5 72.6 all-reduce.10
  172.2 32.3 all-reduce.12
  211.1 72.6 all-reduce.8
where the time goes:
time: 292 us
  waiting for transfers between devices  212 us (73%)
  blocking collectives  38.5 us (13%)
  between operations  14 us (5%)
  matrix products  13.9 us (5%)
  local copies, waits for them, and re-layouts  8 us (3%)
  other arithmetic  5.37 us (2%)
    psum x2, waiting for transfers between devices, per_device(): upper, lower = lax.psum((upper, lower), 'smp')  145 us
    psum x2, waiting for transfers between devices, per_device(): upper, lower = lax.psum((upper, lower), 'tex')  66.7 us
    all_gather x1, blocking collectives, per_device(): w_full = lax.all_gather(w_factor, 'smp', axis=0, tiled=True)  32.7 us
    unnamed x14, local copies, waits for them, and re-layouts  6.74 us
  transfers between devices with their start and end apart: 4, of which 4 were waited for; matrix products, arithmetic and copies ran while one was open for 0% of the time, Pallas kernels for 0%

commit v1 on v0

v1 whole, which is shorter than its diff:
```python
import functools

import jax
import jax.numpy as jnp
from jax import lax
from jax.experimental import pallas as pl
from jax.experimental.pallas import tpu as pltpu
from jax.sharding import PartitionSpec as P

ITERS = 2
MESH = pl.DeviceIdType.MESH
LANES = 128
ROW_ROW = (((1,), (0,)), ((), ()))
LAST_LAST = (((1,), (1,)), ((), ()))


def halves(x):
    high = x.astype(jnp.bfloat16)
    low = (x - high.astype(jnp.float32)).astype(jnp.bfloat16)
    return high, low


def dot3(a, b, dims):
    def one(x, y):
        return lax.dot_general(x, y, dims, preferred_element_type=jnp.float32)

    return one(a[0], b[0]) + (one(a[0], b[1]) + one(a[1], b[0]))


def weight(place, c):
    return (1 - jnp.minimum(jnp.abs(place - c), 1)).astype(jnp.float32)


def put_rows(buf, x, lanes):
    parts, rows, _ = buf.shape
    if rows % 8 == 0:
        buf[:, :, lanes] = x.reshape(parts, rows, x.shape[1])
    else:
        for p in range(parts):
            buf[p, :, lanes] = x[p * rows : (p + 1) * rows]


def get_rows(full, buf):
    parts, rows, _ = buf.shape
    for p in range(parts):
        full[p * rows : (p + 1) * rows, :] = buf[p]


def kernel(
    sizes, listing, values_hbm, w_in, h_in, w_out, h_out,
    values, high, low, note, tex_note, smp_note, tex_list, smp_list,
    w_buf, h_buf, w_full, h_full, h_send, h_recv, w_send, w_recv, h_new, w_new,
    send_t, recv_t, send_s, recv_s, local,
):
    n_tex, n_smp = sizes
    cap, block, _ = values.shape
    rank, texels = w_full.shape[1:]
    samples = h_full.shape[2]
    me_t, me_s = lax.axis_index("tex"), lax.axis_index("smp")
    axes = {
        "tex": (me_t, n_tex, send_t, recv_t),
        "smp": (me_s, n_smp, send_s, recv_s),
    }

    fetch = pltpu.make_async_copy(values_hbm, values, local.at[0])
    fetch.start()

    barrier = pltpu.get_barrier_semaphore()
    for axis, (me, n, _, _) in axes.items():
        for d in range(1, n):
            pl.semaphore_signal(
                barrier, inc=1, device_id={axis: lax.rem(me + d, n)}, device_id_type=MESH
            )

    lane = lax.broadcasted_iota(jnp.int32, (1, LANES), 1)
    text = jnp.full((1, LANES), -1, jnp.int32)
    for side in range(2):
        for j in range(cap):
            text = jnp.where(lane == side * cap + j, listing[side, j], text)
    note[...] = text
    tex_note[me_t] = text
    smp_note[me_s] = text
    w_buf[0, me_s] = w_in[...]
    h_buf[0, me_t] = h_in[...]

    pl.semaphore_wait(barrier, n_tex + n_smp - 2)

    started = []

    def send(axis, phase, source_of, target):
        me, n, send_sem, recv_sem = axes[axis]
        copies = []
        for d in range(1, n):
            to = lax.rem(me + d, n)
            copy = pltpu.make_async_remote_copy(
                src_ref=source_of(to),
                dst_ref=target.at[me],
                send_sem=send_sem.at[phase, d - 1],
                recv_sem=recv_sem.at[phase, d - 1],
                device_id={axis: to},
                device_id_type=MESH,
            )
            copy.start()
            copies.append(copy)
        started.extend(copies)
        return copies

    def arrive(copies):
        for copy in copies:
            copy.wait_recv()

    w_come = send("smp", 0, lambda to: w_in, w_buf.at[0])
    h_come = send("tex", 0, lambda to: h_in, h_buf.at[0])
    notes = send("smp", 1, lambda to: note, smp_note) + send("tex", 1, lambda to: note, tex_note)

    fetch.wait()
    for j in range(cap):
        high[j], low[j] = halves(values[j])
    arrive(notes)
    copies = [
        pltpu.make_async_copy(tex_note, tex_list, local.at[1]),
        pltpu.make_async_copy(smp_note, smp_list, local.at[2]),
    ]
    for copy in copies:
        copy.start()
    for copy in copies:
        copy.wait()
    arrive(w_come)
    get_rows(w_full.at[0], w_buf.at[0])

    def slot_terms(full, side, dims, out):
        for j in range(cap):
            part = None
            for c in range(full.shape[1] // block):
                term = weight(listing[side, j], c) * full[:, c * block : (c + 1) * block]
                part = term if part is None else part + term
            part = halves(part)
            put_rows(out, dot3(part, (high[j], low[j]), dims), slice(j * block, (j + 1) * block))
            gram = dot3(part, part, LAST_LAST)
            first = cap * block + j * rank
            put_rows(out, gram, slice(first, first + rank))

    def updated(own, full, recv, lists, side):
        parts = recv.shape[0]
        count = own.shape[1] // block
        new = []
        for c in range(count):
            upper = gram = None
            for p in range(parts):
                for j in range(cap):
                    hit = weight(lists[p, 0, side * cap + j], c)
                    first = cap * block + j * rank
                    u = hit * recv[p, :, j * block : (j + 1) * block]
                    g = hit * recv[p, :, first : first + rank]
                    upper = u if upper is None else upper + u
                    gram = g if gram is None else gram + g
            where = slice(c * block, (c + 1) * block)
            lower = dot3(halves(gram), halves(full[:, where]), ROW_ROW)
            new.append(own[:, where] * upper / lower)
        return jnp.concatenate(new, axis=1)

    h_own, w_own = h_in[...], w_in[...]
    for sweep in range(ITERS):
        phase = 2 + 2 * sweep
        slot_terms(w_full.at[sweep], 0, ROW_ROW, h_send.at[sweep])
        come = send("tex", phase, lambda to: h_send.at[sweep, to], h_recv.at[sweep])
        h_recv[sweep, me_t] = h_send[sweep, me_t]
        if sweep == 0:
            arrive(h_come)
            get_rows(h_full.at[0], h_buf.at[0])
        arrive(come)
        h_own = updated(h_own, h_full.at[sweep], h_recv.at[sweep], tex_list, 1)
        h_new[sweep] = h_own
        come = send("tex", phase + 1, lambda to: h_new.at[sweep], h_buf.at[sweep + 1])
        h_buf[sweep + 1, me_t] = h_own
        arrive(come)
        get_rows(h_full.at[sweep + 1], h_buf.at[sweep + 1])

        slot_terms(h_full.at[sweep + 1], 1, LAST_LAST, w_send.at[sweep])
        come = send("smp", phase, lambda to: w_send.at[sweep, to], w_recv.at[sweep])
        w_recv[sweep, me_s] = w_send[sweep, me_s]
        arrive(come)
        w_own = updated(w_own, w_full.at[sweep], w_recv.at[sweep], smp_list, 0)
        if sweep < ITERS - 1:
            w_new[sweep] = w_own
            come = send("smp", phase + 1, lambda to: w_new.at[sweep], w_buf.at[sweep + 1])
            w_buf[sweep + 1, me_s] = w_own
            arrive(come)
            get_rows(w_full.at[sweep + 1], w_buf.at[sweep + 1])
    h_out[...] = h_own
    w_out[...] = w_own
    for copy in started:
        copy.wait_send()


def per_device(n_tex, n_smp, blocks, observed, w_factor, h_factor):
    cap = blocks.shape[3]
    block = observed.shape[3]
    w_rows, texels = w_factor.shape
    h_rows, samples = h_factor.shape
    rank = w_rows * n_smp
    wide = cap * block + -(-cap * rank // LANES) * LANES
    phases = 2 + 2 * ITERS
    f32, vmem = jnp.float32, pltpu.VMEM
    dma = pltpu.SemaphoreType.DMA
    return pl.pallas_call(
        functools.partial(kernel, (n_tex, n_smp)),
        out_shape=(
            jax.ShapeDtypeStruct(w_factor.shape, f32),
            jax.ShapeDtypeStruct(h_factor.shape, f32),
        ),
        in_specs=[
            pl.BlockSpec(memory_space=pltpu.SMEM),
            pl.BlockSpec(memory_space=pl.ANY),
            pl.BlockSpec(memory_space=vmem),
            pl.BlockSpec(memory_space=vmem),
        ],
        out_specs=(pl.BlockSpec(memory_space=vmem),) * 2,
        scratch_shapes=[
            vmem((cap, block, block), f32),
            vmem((cap, block, block), jnp.bfloat16),
            vmem((cap, block, block), jnp.bfloat16),
            vmem((1, LANES), jnp.int32),
            vmem((n_tex, 1, LANES), jnp.int32),
            vmem((n_smp, 1, LANES), jnp.int32),
            pltpu.SMEM((n_tex, 1, LANES), jnp.int32),
            pltpu.SMEM((n_smp, 1, LANES), jnp.int32),
            vmem((ITERS, n_smp, w_rows, texels), f32),
            vmem((ITERS + 1, n_tex, h_rows, samples), f32),
            vmem((ITERS, rank, texels), f32),
            vmem((ITERS + 1, rank, samples), f32),
            vmem((ITERS, n_tex, h_rows, wide), f32),
            vmem((ITERS, n_tex, h_rows, wide), f32),
            vmem((ITERS, n_smp, w_rows, wide), f32),
            vmem((ITERS, n_smp, w_rows, wide), f32),
            vmem((ITERS, h_rows, samples), f32),
            vmem((ITERS, w_rows, texels), f32),
            dma((phases, n_tex - 1)),
            dma((phases, n_tex - 1)),
            dma((phases, n_smp - 1)),
            dma((phases, n_smp - 1)),
            dma((3,)),
        ],
        compiler_params=pltpu.CompilerParams(
            collective_id=0, has_side_effects=True, vmem_limit_bytes=40 * 2**20
        ),
    )(
        blocks.reshape(blocks.shape[2:]),
        observed.reshape(cap, block, block),
        w_factor,
        h_factor,
    )


def solution(mesh):
    in_specs = (
        P("tex", "smp", None, None),
        P("tex", "smp", None, None),
        P("smp", "tex"),
        P("tex", "smp"),
    )
    out_specs = (P("smp", "tex"), P("tex", "smp"))
    return jax.shard_map(
        functools.partial(per_device, mesh.shape["tex"], mesh.shape["smp"]),
        mesh=mesh,
        in_specs=in_specs,
        out_specs=out_specs,
        check_vma=False,
    )
```

time: 292 us -> 56.3 us (0.19)
  waiting for transfers between devices: 212 us -> 0 us
  Pallas kernels: 0 us -> 50.8 us
  blocking collectives: 38.5 us -> 0 us
  matrix products: 13.9 us -> 0 us
  between operations: 14 us -> 0.65 us
  other arithmetic: 5.37 us -> 0 us
  local copies, waits for them, and re-layouts: 8 us -> 4.56 us
    psum x4 -> x0, waiting for transfers between devices: 212 us -> none  [the longest x2 145 us: per_device(): upper, lower = lax.psum((upper, lower), 'smp')]
    pallas_call x0 -> x1, Pallas kernels: none -> 50.8 us  [per_device(): pl.pallas_call(functools.partial(kernel, (n_tex, n_smp)), out_shape=(jax....]
    all_gather x2 -> x0, blocking collectives: 38.5 us -> none  [the longest x1 32.7 us: per_device(): w_full = lax.all_gather(w_factor, 'smp', axis=0, tiled=True)]
    dot_general x25 -> x0, matrix products: 13.9 us -> none  [the longest x4 2.5 us: block_factors(): approx = jnp.einsum('ska,skb->sab', w_blocks, h_blocks, precision=highest)]
    div x4 -> x0, other arithmetic: 4.62 us -> none  [the longest x2 2.47 us: per_device(): w_full = w_full * upper / lower]
    unnamed x14 -> x10, local copies, waits for them, and re-layouts: 6.74 us -> 4.56 us
  transfers between devices with their start and end apart: 4 -> 0, of which waited for: 4 -> 0; matrix products, arithmetic and copies ran while one was open for 0% -> 0% of each run, Pallas kernels for 0% -> 0%
where the time goes in v1:
time: 56.3 us; the launch traced here: 56 us
  Pallas kernels  50.8 us (90%)
  local copies, waits for them, and re-layouts  4.56 us (8%)
  between operations  0.65 us (1%)
    pallas_call x1, Pallas kernels, per_device(): pl.pallas_call(functools.partial(kernel, (n_tex, n_smp)), out_shape=(jax....  50.8 us
    unnamed x10, local copies, waits for them, and re-layouts  4.56 us

profile of v1, /device:TPU:0, one launch (start us, length us, event | category | flops | bytes accessed | tf_op | source)
XLA Modules:
  0.0 56.0 jit_solution(5346388933970013465)
XLA Ops:
  0.6 0.0 copy-start.3
  0.6 0.7 %copy-done.3 = s32[1,1,2,2]{3,2,1,0:T(2,128)S(1)} copy-done((s32[1,1,2,2]{3,2,1,0:T(2,128)S(1)}, s32[1,1,2,2]{3,2,1,0:T(2,128)}, u32[]{:S(2)}) %copy-start.3) | copy-done | bytes 40
  1.3 0.0 copy-start
  1.3 1.0 %copy-done = f32[1,1,512,256]{3,2,1,0:T(8,128)S(1)} copy-done((f32[1,1,512,256]{3,2,1,0:T(8,128)S(1)}, f32[1,1,512,256]{3,2,1,0:T(8,128)}, u32[]{:S(2)}) %copy-start) | copy-done | bytes 524312
  2.4 0.0 copy-start.1
  2.4 0.8 %copy-done.1 = f32[16,1024]{1,0:T(8,128)S(1)} copy-done((f32[16,1024]{1,0:T(8,128)S(1)}, f32[16,1024]{1,0:T(8,128)}, u32[]{:S(2)}) %copy-start.1) | copy-done | bytes 65560
  3.2 0.0 copy-start.2
  3.2 0.8 %copy-done.2 = f32[8,1024]{1,0:T(8,128)S(1)} copy-done((f32[8,1024]{1,0:T(8,128)S(1)}, f32[8,1024]{1,0:T(8,128)}, u32[]{:S(2)}) %copy-start.2) | copy-done | bytes 32792
  4.0 50.8 %shard_map.59 = (f32[8,1024]{1,0:T(8,128)S(1)}, f32[16,1024]{1,0:T(8,128)S(1)}) custom-call(s32[2,2]{1,0:T(2,128)S(1)} %bitcast.3, f32[2,256,256]{2,1,0:T(8,128)S(1)} %bitcast.2, f32[8,1024]{1,0:T(8,128)S(1)} %copy-done.2, f32[16,1024]{1,0:T(8,128)S(1)} %copy-done.1), custom_call_target="tpu_custom_call" | custom-call | tf_op jit(solution)/shard_map/pallas_call | solution.py:206
  54.7 0.6 %copy.8 = f32[8,1024]{1,0:T(8,128)} copy(f32[8,1024]{1,0:T(8,128)S(1)} %get-tuple-element.4) | data formatting | bytes 65536
  55.3 0.6 %copy.9 = f32[16,1024]{1,0:T(8,128)} copy(f32[16,1024]{1,0:T(8,128)S(1)} %get-tuple-element.5) | data formatting | bytes 131072
Async XLA Ops:
  0.6 0.7 %copy-start.3 = (s32[1,1,2,2]{3,2,1,0:T(2,128)S(1)}, s32[1,1,2,2]{3,2,1,0:T(2,128)}, u32[]{:S(2)}) copy-start(s32[1,1,2,2]{3,2,1,0:T(2,128)} %param.4) | copy-start | bytes 52
  1.3 1.0 %copy-start = (f32[1,1,512,256]{3,2,1,0:T(8,128)S(1)}, f32[1,1,512,256]{3,2,1,0:T(8,128)}, u32[]{:S(2)}) copy-start(f32[1,1,512,256]{3,2,1,0:T(8,128)} %param.5) | copy-start | bytes 1572868
  2.4 0.8 %copy-start.1 = (f32[16,1024]{1,0:T(8,128)S(1)}, f32[16,1024]{1,0:T(8,128)}, u32[]{:S(2)}) copy-start(f32[16,1024]{1,0:T(8,128)} %h_in.1) | copy-start | bytes 196612
  3.2 0.8 %copy-start.2 = (f32[8,1024]{1,0:T(8,128)S(1)}, f32[8,1024]{1,0:T(8,128)}, u32[]{:S(2)}) copy-start(f32[8,1024]{1,0:T(8,128)} %w_in.1) | copy-start | bytes 98308

commit v2 on v1

v2 whole, which is shorter than its diff:
```python
import functools

import jax
import jax.numpy as jnp
from jax import lax
from jax.experimental import pallas as pl
from jax.experimental.pallas import tpu as pltpu
from jax.sharding import PartitionSpec as P

ITERS = 2
MESH = pl.DeviceIdType.MESH
LANES = 128
ROW_ROW = (((1,), (0,)), ((), ()))
LAST_LAST = (((1,), (1,)), ((), ()))


def halves(x):
    high = x.astype(jnp.bfloat16)
    low = (x - high.astype(jnp.float32)).astype(jnp.bfloat16)
    return high, low


def dot(a, b, dims=ROW_ROW):
    return lax.dot_general(a, b, dims, preferred_element_type=jnp.float32)


def weight(place, c):
    return (1 - jnp.minimum(jnp.abs(place - c), 1)).astype(jnp.float32)


def put_rows(buf, x, lanes):
    parts, rows, _ = buf.shape
    if rows % 8 == 0:
        buf[:, :, lanes] = x.reshape(parts, rows, x.shape[1])
    else:
        for p in range(parts):
            buf[p, :, lanes] = x[p * rows : (p + 1) * rows]


def get_rows(full, buf):
    parts, rows, _ = buf.shape
    for p in range(parts):
        full[p * rows : (p + 1) * rows, :] = buf[p]


def kernel(
    sizes, listing_hbm, values_hbm, w_in, h_in, w_out, h_out,
    listing, values, high, low, turned_high, turned_low,
    note, tex_note, smp_note, tex_list, smp_list, tex_hot, smp_hot,
    w_buf, h_buf, w_full, h_full, h_send, h_recv, w_send, w_recv, stack,
    send_t, recv_t, send_s, recv_s, local,
):
    n_tex, n_smp = sizes
    cap, block, _ = values.shape
    rank, texels = w_full.shape
    samples = h_full.shape[1]
    me_t, me_s = lax.axis_index("tex"), lax.axis_index("smp")
    axes = {
        "tex": (me_t, n_tex, send_t, recv_t),
        "smp": (me_s, n_smp, send_s, recv_s),
    }

    fetch = [
        pltpu.make_async_copy(w_in, w_buf.at[0, me_s], local.at[0]),
        pltpu.make_async_copy(h_in, h_buf.at[0, me_t], local.at[1]),
        pltpu.make_async_copy(listing_hbm, listing, local.at[2]),
        pltpu.make_async_copy(values_hbm, values, local.at[3]),
    ]
    for copy in fetch:
        copy.start()

    barrier = pltpu.get_barrier_semaphore()
    for axis, (me, n, _, _) in axes.items():
        for d in range(1, n):
            pl.semaphore_signal(
                barrier, inc=1, device_id={axis: lax.rem(me + d, n)}, device_id_type=MESH
            )
    for copy in fetch[:3]:
        copy.wait()
    lane = lax.broadcasted_iota(jnp.int32, (1, LANES), 1)
    text = jnp.full((1, LANES), -1, jnp.int32)
    for side in range(2):
        for j in range(cap):
            text = jnp.where(lane == side * cap + j, listing[side, j], text)
    note[...] = text
    tex_note[me_t] = text
    smp_note[me_s] = text

    pl.semaphore_wait(barrier, n_tex + n_smp - 2)

    started = []

    def push(axis, phase, at, src, dst, to):
        _, _, send_sem, recv_sem = axes[axis]
        copy = pltpu.make_async_remote_copy(
            src_ref=src,
            dst_ref=dst,
            send_sem=send_sem.at[phase, at],
            recv_sem=recv_sem.at[phase, at],
            device_id={axis: to},
            device_id_type=MESH,
        )
        copy.start()
        started.append(copy)
        return copy

    def scatter(axis, phase, source_of, target):
        me, n, _, _ = axes[axis]
        copies = []
        for d in range(1, n):
            to = lax.rem(me + d, n)
            copies.append(push(axis, phase, d - 1, source_of(to), target, to))
        return copies

    def gather_begin(axis, phase, buf):
        me, n, _, _ = axes[axis]
        mine = buf.at[me]
        copies = []
        for d in range(1, n // 2):
            copies.append(push(axis, phase, d - 1, mine, mine, lax.rem(me + 2 * d, n)))
        mate = me + 1 - 2 * lax.rem(me, 2)
        copies.append(push(axis, phase, n // 2 - 1, mine, mine, mate))
        return copies

    def gather_forward(axis, phase, buf, copies):
        me, n, _, _ = axes[axis]
        mate = me + 1 - 2 * lax.rem(me, 2)
        late = copies[-1:]
        for d in range(1, n // 2):
            copies[d - 1].wait_recv()
            came = buf.at[lax.rem(me + n - 2 * d, n)]
            late.append(push(axis, phase, n // 2 - 1 + d, came, came, mate))
        return late

    def arrive(copies):
        for copy in copies:
            copy.wait_recv()

    w_come = gather_begin("smp", 0, w_buf.at[0])
    h_come = gather_begin("tex", 0, h_buf.at[0])
    notes = scatter("smp", 1, lambda to: note, smp_note.at[me_s])
    notes += scatter("tex", 1, lambda to: note, tex_note.at[me_t])

    h_come = gather_forward("tex", 0, h_buf.at[0], h_come)
    w_come = gather_forward("smp", 0, w_buf.at[0], w_come)
    arrive(notes)
    copies = [
        pltpu.make_async_copy(tex_note, tex_list, local.at[4]),
        pltpu.make_async_copy(smp_note, smp_list, local.at[5]),
    ]
    for copy in copies:
        copy.start()
    fetch[3].wait()
    for j in range(cap):
        high[j], low[j] = halves(values[j])
        turned_high[j], turned_low[j] = halves(values[j].T)
    arrive(w_come)
    get_rows(w_full, w_buf.at[0])

    def slot_terms(full, side, weights, out, send):
        parts = []
        edge = cap * block
        for j in range(cap):
            part = None
            for c in range(full.shape[1] // block):
                term = weight(listing[side, j], c) * full[:, c * block : (c + 1) * block]
                part = term if part is None else part + term
            parts.append(halves(part))
            both = jnp.concatenate(parts[j], axis=0)
            twice = dot(both, weights[0][j])
            upper = twice[:rank] + (twice[rank:] + dot(parts[j][0], weights[1][j]))
            put_rows(out, upper, slice(j * block, (j + 1) * block))
            if j == cap - 2:
                come = send(0, pl.ds(0, edge - block))
        for j in range(cap):
            both = jnp.concatenate(parts[j], axis=0)
            twice = dot(both, parts[j][0], LAST_LAST)
            gram = twice[:rank] + (twice[rank:] + dot(parts[j][0], parts[j][1], LAST_LAST))
            put_rows(out, gram, slice(edge + j * rank, edge + (j + 1) * rank))
        return come + send(1, pl.ds(edge - block, out.shape[2] - edge + block))

    def stack_up(full):
        part = halves(full[...])
        stack[:rank, : full.shape[1]] = part[0]
        stack[rank : 2 * rank, : full.shape[1]] = part[1]
        stack[2 * rank :, : full.shape[1]] = part[0]

    def updated(own, recv, hot):
        parts = recv.shape[0]
        count = own.shape[1] // block
        new = []
        for c in range(count):
            upper = gram = None
            for p in range(parts):
                for j in range(cap):
                    hit = hot[(p * cap + j) * count + c]
                    first = cap * block + j * rank
                    u = hit * recv[p, :, j * block : (j + 1) * block]
                    g = hit * recv[p, :, first : first + rank]
                    upper = u if upper is None else upper + u
                    gram = g if gram is None else gram + g
            where = slice(c * block, (c + 1) * block)
            g_high, g_low = halves(gram)
            lower = dot(jnp.concatenate([g_high, g_high, g_low], axis=1), stack[:, where])
            new.append(own[:, where] * upper / lower)
        return jnp.concatenate(new, axis=1)

    def sender(axis, sweep, out, target):
        me = axes[axis][0]

        def send(half, lanes):
            return scatter(
                axis, 2 + 3 * sweep + half,
                lambda to: out.at[to, :, lanes], target.at[me, :, lanes],
            )

        return send

    h_own, w_own = h_buf[0, me_t], w_buf[0, me_s]
    for sweep in range(ITERS):
        out, target = h_send.at[sweep], h_recv.at[sweep]
        come = slot_terms(w_full, 0, (high, low), out, sender("tex", sweep, out, target))
        h_recv[sweep, me_t] = h_send[sweep, me_t]
        if sweep == 0:
            for copy in copies:
                copy.wait()
            for lists, hot, n, side in ((tex_list, tex_hot, n_tex, 1), (smp_list, smp_hot, n_smp, 0)):
                count = (texels, samples)[side] // block
                for p in range(n):
                    for j in range(cap):
                        for c in range(count):
                            hot[(p * cap + j) * count + c] = weight(lists[p, 0, side * cap + j], c)
            arrive(h_come)
            get_rows(h_full, h_buf.at[0])
        stack_up(h_full)
        arrive(come)
        h_own = updated(h_own, h_recv.at[sweep], tex_hot)
        h_buf[sweep + 1, me_t] = h_own
        buf, phase = h_buf.at[sweep + 1], 4 + 3 * sweep
        come = gather_begin("tex", phase, buf)
        stack_up(w_full)
        arrive(gather_forward("tex", phase, buf, come))
        get_rows(h_full, buf)

        out, target = w_send.at[sweep], w_recv.at[sweep]
        come = slot_terms(
            h_full, 1, (turned_high, turned_low), out, sender("smp", sweep, out, target)
        )
        w_recv[sweep, me_s] = w_send[sweep, me_s]
        arrive(come)
        w_own = updated(w_own, w_recv.at[sweep], smp_hot)
        if sweep < ITERS - 1:
            w_buf[sweep + 1, me_s] = w_own
            buf = w_buf.at[sweep + 1]
            come = gather_begin("smp", phase, buf)
            arrive(gather_forward("smp", phase, buf, come))
            get_rows(w_full, buf)
    h_out[...] = h_own
    w_out[...] = w_own
    for copy in started:
        copy.wait_send()


def per_device(n_tex, n_smp, blocks, observed, w_factor, h_factor):
    cap = blocks.shape[3]
    block = observed.shape[3]
    w_rows, texels = w_factor.shape
    h_rows, samples = h_factor.shape
    rank = w_rows * n_smp
    wide = cap * block + -(-cap * rank // LANES) * LANES
    phases = 2 + 3 * ITERS
    f32, half, vmem = jnp.float32, jnp.bfloat16, pltpu.VMEM
    dma = pltpu.SemaphoreType.DMA
    return pl.pallas_call(
        functools.partial(kernel, (n_tex, n_smp)),
        out_shape=(
            jax.ShapeDtypeStruct(w_factor.shape, f32),
            jax.ShapeDtypeStruct(h_factor.shape, f32),
        ),
        in_specs=[pl.BlockSpec(memory_space=pl.ANY)] * 4,
        out_specs=(pl.BlockSpec(memory_space=vmem),) * 2,
        scratch_shapes=[
            pltpu.SMEM(blocks.shape[2:], jnp.int32),
            vmem((cap, block, block), f32),
            vmem((cap, block, block), half),
            vmem((cap, block, block), half),
            vmem((cap, block, block), half),
            vmem((cap, block, block), half),
            vmem((1, LANES), jnp.int32),
            vmem((n_tex, 1, LANES), jnp.int32),
            vmem((n_smp, 1, LANES), jnp.int32),
            pltpu.SMEM((n_tex, 1, LANES), jnp.int32),
            pltpu.SMEM((n_smp, 1, LANES), jnp.int32),
            pltpu.SMEM((n_tex * cap * (samples // block),), f32),
            pltpu.SMEM((n_smp * cap * (texels // block),), f32),
            vmem((ITERS, n_smp, w_rows, texels), f32),
            vmem((ITERS + 1, n_tex, h_rows, samples), f32),
            vmem((rank, texels), f32),
            vmem((rank, samples), f32),
            vmem((ITERS, n_tex, h_rows, wide), f32),
            vmem((ITERS, n_tex, h_rows, wide), f32),
            vmem((ITERS, n_smp, w_rows, wide), f32),
            vmem((ITERS, n_smp, w_rows, wide), f32),
            vmem((3 * rank, max(texels, samples)), half),
            dma((phases, n_tex - 1)),
            dma((phases, n_tex - 1)),
            dma((phases, n_smp - 1)),
            dma((phases, n_smp - 1)),
            dma((6,)),
        ],
        compiler_params=pltpu.CompilerParams(
            collective_id=0, has_side_effects=True, vmem_limit_bytes=60 * 2**20
        ),
    )(
        blocks.reshape(blocks.shape[2:]),
        observed.reshape(cap, block, block),
        w_factor,
        h_factor,
    )


def solution(mesh):
    in_specs = (
        P("tex", "smp", None, None),
        P("tex", "smp", None, None),
        P("smp", "tex"),
        P("tex", "smp"),
    )
    out_specs = (P("smp", "tex"), P("tex", "smp"))
    return jax.shard_map(
        functools.partial(per_device, mesh.shape["tex"], mesh.shape["smp"]),
        mesh=mesh,
        in_specs=in_specs,
        out_specs=out_specs,
        check_vma=False,
    )
```

time: 56.3 us -> 53.6 us (0.952)
  local copies, waits for them, and re-layouts: 4.56 us -> 2.04 us
    unnamed x10 -> x4, local copies, waits for them, and re-layouts: 4.56 us -> 2.04 us
where the time goes in v2:
time: 53.6 us; the launch traced here: 53.4 us
  Pallas kernels  50.8 us (95%)
  local copies, waits for them, and re-layouts  2.04 us (4%)
  between operations  0.65 us (1%)
    pallas_call x1, Pallas kernels, per_device(): pl.pallas_call(functools.partial(kernel, (n_tex, n_smp)), out_shape=(jax....  50.8 us
    unnamed x4, local copies, waits for them, and re-layouts  2.04 us

profile of v2, /device:TPU:0, one launch (start us, length us, event | category | flops | bytes accessed | tf_op | source)
XLA Modules:
  0.0 53.4 jit_solution(13363702505957874019)
XLA Ops:
  0.6 50.8 %shard_map.59 = (f32[8,1024]{1,0:T(8,128)}, f32[16,1024]{1,0:T(8,128)}) custom-call(s32[2,2]{1,0:T(2,128)} %bitcast.3, f32[2,256,256]{2,1,0:T(8,128)} %bitcast.2, f32[8,1024]{1,0:T(8,128)} %w_in.1, f32[16,1024]{1,0:T(8,128)} %h_in.1), custom_call_target="tpu_custom_call" | custom-call | tf_op jit(solution)/shard_map/pallas_call | solution.py:274
  51.4 0.0 copy-start
  51.4 1.4 %copy.8 = f32[8,1024]{1,0:T(8,128)} copy(f32[8,1024]{1,0:T(8,128)} %get-tuple-element.4) | data formatting | bytes 65536
  52.8 0.0 copy-done
  52.8 0.6 %copy.9 = f32[16,1024]{1,0:T(8,128)} copy(f32[16,1024]{1,0:T(8,128)S(1)} %copy-done) | data formatting | bytes 131072
Async XLA Ops:
  51.4 1.4 %copy-start = (f32[16,1024]{1,0:T(8,128)S(1)}, f32[16,1024]{1,0:T(8,128)}, u32[]{:S(2)}) copy-start(f32[16,1024]{1,0:T(8,128)} %get-tuple-element.5) | copy-start | bytes 196612

commit v3 on v2

--- a/solution.py
+++ b/solution.py
@@ -47,7 +47,8 @@
     sizes, listing_hbm, values_hbm, w_in, h_in, w_out, h_out,
     listing, values, high, low, turned_high, turned_low,
     note, tex_note, smp_note, tex_list, smp_list, tex_hot, smp_hot,
-    w_buf, h_buf, w_full, h_full, h_send, h_recv, w_send, w_recv, stack,
+    w_buf, h_buf, w_full, h_full, h_send, h_recv, w_send, w_recv,
+    h_pick, h_picked, w_pick, w_picked, h_part, w_part, h_last, w_last, stack,
     send_t, recv_t, send_s, recv_s, local,
 ):
     n_tex, n_smp = sizes
@@ -157,15 +158,26 @@
     arrive(w_come)
     get_rows(w_full, w_buf.at[0])
 
-    def slot_terms(full, side, weights, out, send):
+    def part_of_full(full, side, j):
+        part = None
+        for c in range(full.shape[1] // block):
+            term = weight(listing[side, j], c) * full[:, c * block : (c + 1) * block]
+            part = term if part is None else part + term
+        return part
+
+    def part_of_picked(picked, spare, j):
+        where = slice(j * block, (j + 1) * block)
+        if picked.shape[1] % 8 == 0:
+            return picked[:, :, where].reshape(rank, block)
+        if j == 0:
+            get_rows(spare, picked)
+        return spare[:, where]
+
+    def slot_terms(part_of, weights, out, send):
         parts = []
         edge = cap * block
         for j in range(cap):
-            part = None
-            for c in range(full.shape[1] // block):
-                term = weight(listing[side, j], c) * full[:, c * block : (c + 1) * block]
-                part = term if part is None else part + term
-            parts.append(halves(part))
+            parts.append(halves(part_of(j)))
             both = jnp.concatenate(parts[j], axis=0)
             twice = dot(both, weights[0][j])
             upper = twice[:rank] + (twice[rank:] + dot(parts[j][0], weights[1][j]))
@@ -185,32 +197,53 @@
         stack[rank : 2 * rank, : full.shape[1]] = part[1]
         stack[2 * rank :, : full.shape[1]] = part[0]
 
-    def updated(own, recv, hot):
-        parts = recv.shape[0]
+    def updated(axis, own, recv, hot, come):
+        me, n, _, _ = axes[axis]
         count = own.shape[1] // block
+        upper, gram = [None] * count, [None] * count
+        for d in range(n):
+            p = lax.rem(me + n - d, n)
+            if d > 0:
+                arrive([come[d - 1], come[n - 1 + d - 1]])
+            for j in range(cap):
+                first = cap * block + j * rank
+                u = recv[p, :, j * block : (j + 1) * block]
+                g = recv[p, :, first : first + rank]
+                for c in range(count):
+                    hit = hot[(p * cap + j) * count + c]
+                    upper[c] = hit * u if upper[c] is None else upper[c] + hit * u
+                    gram[c] = hit * g if gram[c] is None else gram[c] + hit * g
         new = []
         for c in range(count):
-            upper = gram = None
-            for p in range(parts):
-                for j in range(cap):
-                    hit = hot[(p * cap + j) * count + c]
-                    first = cap * block + j * rank
-                    u = hit * recv[p, :, j * block : (j + 1) * block]
-                    g = hit * recv[p, :, first : first + rank]
-                    upper = u if upper is None else upper + u
-                    gram = g if gram is None else gram + g
             where = slice(c * block, (c + 1) * block)
-            g_high, g_low = halves(gram)
+            g_high, g_low = halves(gram[c])
             lower = dot(jnp.concatenate([g_high, g_high, g_low], axis=1), stack[:, where])
-            new.append(own[:, where] * upper / lower)
+            new.append(own[:, where] * upper[c] / lower)
         return jnp.concatenate(new, axis=1)
+
+    def send_picked(axis, phase, new, hot, pick, picked):
+        me, n, _, _ = axes[axis]
+        count = new.shape[1] // block
+        copies = []
+        for d in list(range(1, n)) + [0]:
+            to = lax.rem(me + d, n)
+            for j in range(cap):
+                part = None
+                for c in range(count):
+                    hit = hot[(to * cap + j) * count + c]
+                    term = hit * new[:, c * block : (c + 1) * block]
+                    part = term if part is None else part + term
+                (pick if d else picked)[to, :, j * block : (j + 1) * block] = part
+            if d:
+                copies.append(push(axis, phase, d - 1, pick.at[to], picked.at[me], to))
+        return copies
 
     def sender(axis, sweep, out, target):
         me = axes[axis][0]
 
         def send(half, lanes):
             return scatter(
-                axis, 2 + 3 * sweep + half,
+                axis, 2 + 4 * sweep + half,
                 lambda to: out.at[to, :, lanes], target.at[me, :, lanes],
             )
 
@@ -218,8 +251,15 @@
 
     h_own, w_own = h_buf[0, me_t], w_buf[0, me_s]
     for sweep in range(ITERS):
+        phase = 4 + 4 * sweep
+        more = sweep < ITERS - 1
         out, target = h_send.at[sweep], h_recv.at[sweep]
-        come = slot_terms(w_full, 0, (high, low), out, sender("tex", sweep, out, target))
+        send = sender("tex", sweep, out, target)
+        if sweep == 0:
+            part_of = functools.partial(part_of_full, w_full, 0)
+        else:
+            part_of = functools.partial(part_of_picked, w_picked.at[sweep - 1], w_part)
+        come = slot_terms(part_of, (high, low), out, send)
         h_recv[sweep, me_t] = h_send[sweep, me_t]
         if sweep == 0:
             for copy in copies:
@@ -230,35 +270,46 @@
                     for j in range(cap):
                         for c in range(count):
                             hot[(p * cap + j) * count + c] = weight(lists[p, 0, side * cap + j], c)
-            arrive(h_come)
-            get_rows(h_full, h_buf.at[0])
+        else:
+            mine = w_buf.at[sweep, me_s]
+            w_come = scatter("smp", phase + 1, lambda to: mine, mine)
+        arrive(h_come)
+        get_rows(h_full, h_buf.at[sweep])
         stack_up(h_full)
+        h_own = updated("tex", h_own, h_recv.at[sweep], tex_hot, come)
+        come = send_picked("tex", phase, h_own, tex_hot, h_pick.at[sweep], h_picked.at[sweep])
+        if more:
+            h_buf[sweep + 1, me_t] = h_own
+        else:
+            h_last[...] = h_own
+            h_store = pltpu.make_async_copy(h_last, h_out, local.at[6])
+            h_store.start()
+        if sweep > 0:
+            arrive(w_come)
+            get_rows(w_full, w_buf.at[sweep])
+        stack_up(w_full)
         arrive(come)
-        h_own = updated(h_own, h_recv.at[sweep], tex_hot)
-        h_buf[sweep + 1, me_t] = h_own
-        buf, phase = h_buf.at[sweep + 1], 4 + 3 * sweep
-        come = gather_begin("tex", phase, buf)
-        stack_up(w_full)
-        arrive(gather_forward("tex", phase, buf, come))
-        get_rows(h_full, buf)
 
         out, target = w_send.at[sweep], w_recv.at[sweep]
-        come = slot_terms(
-            h_full, 1, (turned_high, turned_low), out, sender("smp", sweep, out, target)
-        )
+        send = sender("smp", sweep, out, target)
+        part_of = functools.partial(part_of_picked, h_picked.at[sweep], h_part)
+        come = slot_terms(part_of, (turned_high, turned_low), out, send)
         w_recv[sweep, me_s] = w_send[sweep, me_s]
-        arrive(come)
-        w_own = updated(w_own, w_recv.at[sweep], smp_hot)
-        if sweep < ITERS - 1:
+        if more:
+            mine = h_buf.at[sweep + 1, me_t]
+            h_come = scatter("tex", phase + 1, lambda to: mine, mine)
+        w_own = updated("smp", w_own, w_recv.at[sweep], smp_hot, come)
+        if more:
+            come = send_picked("smp", phase, w_own, smp_hot, w_pick.at[sweep], w_picked.at[sweep])
             w_buf[sweep + 1, me_s] = w_own
-            buf = w_buf.at[sweep + 1]
-            come = gather_begin("smp", phase, buf)
-            arrive(gather_forward("smp", phase, buf, come))
-            get_rows(w_full, buf)
-    h_out[...] = h_own
-    w_out[...] = w_own
+            arrive(come)
+    w_last[...] = w_own
+    w_store = pltpu.make_async_copy(w_last, w_out, local.at[7])
+    w_store.start()
     for copy in started:
         copy.wait_send()
+    h_store.wait()
+    w_store.wait()
 
 
 def per_device(n_tex, n_smp, blocks, observed, w_factor, h_factor):
@@ -268,7 +319,7 @@
     h_rows, samples = h_factor.shape
     rank = w_rows * n_smp
     wide = cap * block + -(-cap * rank // LANES) * LANES
-    phases = 2 + 3 * ITERS
+    phases = 2 + 4 * ITERS
     f32, half, vmem = jnp.float32, jnp.bfloat16, pltpu.VMEM
     dma = pltpu.SemaphoreType.DMA
     return pl.pallas_call(
@@ -278,7 +329,7 @@
             jax.ShapeDtypeStruct(h_factor.shape, f32),
         ),
         in_specs=[pl.BlockSpec(memory_space=pl.ANY)] * 4,
-        out_specs=(pl.BlockSpec(memory_space=vmem),) * 2,
+        out_specs=(pl.BlockSpec(memory_space=pl.ANY),) * 2,
         scratch_shapes=[
             pltpu.SMEM(blocks.shape[2:], jnp.int32),
             vmem((cap, block, block), f32),
@@ -294,19 +345,27 @@
             pltpu.SMEM((n_tex * cap * (samples // block),), f32),
             pltpu.SMEM((n_smp * cap * (texels // block),), f32),
             vmem((ITERS, n_smp, w_rows, texels), f32),
-            vmem((ITERS + 1, n_tex, h_rows, samples), f32),
+            vmem((ITERS, n_tex, h_rows, samples), f32),
             vmem((rank, texels), f32),
             vmem((rank, samples), f32),
             vmem((ITERS, n_tex, h_rows, wide), f32),
             vmem((ITERS, n_tex, h_rows, wide), f32),
             vmem((ITERS, n_smp, w_rows, wide), f32),
             vmem((ITERS, n_smp, w_rows, wide), f32),
+            vmem((ITERS, n_tex, h_rows, cap * block), f32),
+            vmem((ITERS, n_tex, h_rows, cap * block), f32),
+            vmem((ITERS, n_smp, w_rows, cap * block), f32),
+            vmem((ITERS, n_smp, w_rows, cap * block), f32),
+            vmem((rank, cap * block), f32),
+            vmem((rank, cap * block), f32),
+            vmem(h_factor.shape, f32),
+            vmem(w_factor.shape, f32),
             vmem((3 * rank, max(texels, samples)), half),
             dma((phases, n_tex - 1)),
             dma((phases, n_tex - 1)),
             dma((phases, n_smp - 1)),
             dma((phases, n_smp - 1)),
-            dma((6,)),
+            dma((8,)),
         ],
         compiler_params=pltpu.CompilerParams(
             collective_id=0, has_side_effects=True, vmem_limit_bytes=60 * 2**20

time: 53.6 us -> 50.1 us (0.935)
  Pallas kernels: 50.8 us -> 47.3 us
    pallas_call x1, Pallas kernels: 50.8 us -> 47.3 us  [per_device(): pl.pallas_call(functools.partial(kernel, (n_tex, n_smp)), out_shape=(jax....]
where the time goes in v3:
time: 50.1 us; the launch traced here: 50 us
  Pallas kernels  47.3 us (94%)
  local copies, waits for them, and re-layouts  2.04 us (4%)
  between operations  0.65 us (1%)
    pallas_call x1, Pallas kernels, per_device(): pl.pallas_call(functools.partial(kernel, (n_tex, n_smp)), out_shape=(jax....  47.3 us
    unnamed x4, local copies, waits for them, and re-layouts  2.04 us

profile of v3, /device:TPU:0, one launch (start us, length us, event | category | flops | bytes accessed | tf_op | source)
XLA Modules:
  0.0 50.0 jit_solution(9810019972413216728)
XLA Ops:
  0.6 47.3 %shard_map.59 = (f32[8,1024]{1,0:T(8,128)}, f32[16,1024]{1,0:T(8,128)}) custom-call(s32[2,2]{1,0:T(2,128)} %bitcast.3, f32[2,256,256]{2,1,0:T(8,128)} %bitcast.2, f32[8,1024]{1,0:T(8,128)} %w_in.1, f32[16,1024]{1,0:T(8,128)} %h_in.1), custom_call_target="tpu_custom_call" | custom-call | tf_op jit(solution)/shard_map/pallas_call | solution.py:325
  47.9 0.0 copy-start
  47.9 1.4 %copy.8 = f32[8,1024]{1,0:T(8,128)} copy(f32[8,1024]{1,0:T(8,128)} %get-tuple-element.4) | data formatting | bytes 65536
  49.3 0.0 copy-done
  49.3 0.6 %copy.9 = f32[16,1024]{1,0:T(8,128)} copy(f32[16,1024]{1,0:T(8,128)S(1)} %copy-done) | data formatting | bytes 131072
Async XLA Ops:
  47.9 1.4 %copy-start = (f32[16,1024]{1,0:T(8,128)S(1)}, f32[16,1024]{1,0:T(8,128)}, u32[]{:S(2)}) copy-start(f32[16,1024]{1,0:T(8,128)} %get-tuple-element.5) | copy-start | bytes 196612

commit v4 on v3

--- a/solution.py
+++ b/solution.py
@@ -48,7 +48,7 @@
     listing, values, high, low, turned_high, turned_low,
     note, tex_note, smp_note, tex_list, smp_list, tex_hot, smp_hot,
     w_buf, h_buf, w_full, h_full, h_send, h_recv, w_send, w_recv,
-    h_pick, h_picked, w_pick, w_picked, h_part, w_part, h_last, w_last, stack,
+    h_pick, h_picked, w_pick, w_picked, h_part, w_part, stack, stack_low,
     send_t, recv_t, send_s, recv_s, local,
 ):
     n_tex, n_smp = sizes
@@ -184,40 +184,54 @@
             put_rows(out, upper, slice(j * block, (j + 1) * block))
             if j == cap - 2:
                 come = send(0, pl.ds(0, edge - block))
+        left = jnp.concatenate([half for pair in parts for half in pair], axis=0)
+        right = jnp.concatenate([pair[0] for pair in parts] + [pair[1] for pair in parts], axis=0)
+        every = dot(left, right, LAST_LAST)
+        span = cap * rank
+        gram = None
         for j in range(cap):
-            both = jnp.concatenate(parts[j], axis=0)
-            twice = dot(both, parts[j][0], LAST_LAST)
-            gram = twice[:rank] + (twice[rank:] + dot(parts[j][0], parts[j][1], LAST_LAST))
-            put_rows(out, gram, slice(edge + j * rank, edge + (j + 1) * rank))
+            top = every[2 * j * rank : (2 * j + 1) * rank]
+            bottom = every[(2 * j + 1) * rank : (2 * j + 2) * rank]
+            own = top[:, :span] + (top[:, span:] + bottom[:, :span])
+            gram = own if gram is None else jnp.where(slot_of(rank) == j, own, gram)
+        put_rows(out, gram, slice(edge, edge + span))
         return come + send(1, pl.ds(edge - block, out.shape[2] - edge + block))
+
+    def slot_of(rows):
+        return lax.broadcasted_iota(jnp.int32, (rows, cap * rank), 1) // rank
 
     def stack_up(full):
         part = halves(full[...])
-        stack[:rank, : full.shape[1]] = part[0]
-        stack[rank : 2 * rank, : full.shape[1]] = part[1]
-        stack[2 * rank :, : full.shape[1]] = part[0]
+        width = full.shape[1]
+        for i in range(2 * cap):
+            stack[i * rank : (i + 1) * rank, :width] = part[0]
+        for i in range(cap):
+            stack_low[i * rank : (i + 1) * rank, :width] = part[1]
 
     def updated(axis, own, recv, hot, come):
         me, n, _, _ = axes[axis]
         count = own.shape[1] // block
         upper, gram = [None] * count, [None] * count
+        slots = slot_of(recv.shape[1])
         for d in range(n):
             p = lax.rem(me + n - d, n)
             if d > 0:
                 arrive([come[d - 1], come[n - 1 + d - 1]])
-            for j in range(cap):
-                first = cap * block + j * rank
-                u = recv[p, :, j * block : (j + 1) * block]
-                g = recv[p, :, first : first + rank]
-                for c in range(count):
+            g = recv[p, :, cap * block : cap * block + cap * rank]
+            for c in range(count):
+                mixed = None
+                for j in range(cap):
                     hit = hot[(p * cap + j) * count + c]
-                    upper[c] = hit * u if upper[c] is None else upper[c] + hit * u
-                    gram[c] = hit * g if gram[c] is None else gram[c] + hit * g
+                    u = hit * recv[p, :, j * block : (j + 1) * block]
+                    upper[c] = u if upper[c] is None else upper[c] + u
+                    mixed = hit if mixed is None else jnp.where(slots == j, hit, mixed)
+                gram[c] = mixed * g if gram[c] is None else gram[c] + mixed * g
         new = []
         for c in range(count):
             where = slice(c * block, (c + 1) * block)
             g_high, g_low = halves(gram[c])
-            lower = dot(jnp.concatenate([g_high, g_high, g_low], axis=1), stack[:, where])
+            lower = dot(jnp.concatenate([g_high, g_low], axis=1), stack[:, where])
+            lower = lower + dot(g_high, stack_low[:, where])
             new.append(own[:, where] * upper[c] / lower)
         return jnp.concatenate(new, axis=1)
 
@@ -281,9 +295,7 @@
         if more:
             h_buf[sweep + 1, me_t] = h_own
         else:
-            h_last[...] = h_own
-            h_store = pltpu.make_async_copy(h_last, h_out, local.at[6])
-            h_store.start()
+            h_out[...] = h_own
         if sweep > 0:
             arrive(w_come)
             get_rows(w_full, w_buf.at[sweep])
@@ -303,13 +315,9 @@
             come = send_picked("smp", phase, w_own, smp_hot, w_pick.at[sweep], w_picked.at[sweep])
             w_buf[sweep + 1, me_s] = w_own
             arrive(come)
-    w_last[...] = w_own
-    w_store = pltpu.make_async_copy(w_last, w_out, local.at[7])
-    w_store.start()
+    w_out[...] = w_own
     for copy in started:
         copy.wait_send()
-    h_store.wait()
-    w_store.wait()
 
 
 def per_device(n_tex, n_smp, blocks, observed, w_factor, h_factor):
@@ -325,11 +333,11 @@
     return pl.pallas_call(
         functools.partial(kernel, (n_tex, n_smp)),
         out_shape=(
-            jax.ShapeDtypeStruct(w_factor.shape, f32),
-            jax.ShapeDtypeStruct(h_factor.shape, f32),
+            pltpu.VMEM(w_factor.shape, f32),
+            pltpu.VMEM(h_factor.shape, f32),
         ),
         in_specs=[pl.BlockSpec(memory_space=pl.ANY)] * 4,
-        out_specs=(pl.BlockSpec(memory_space=pl.ANY),) * 2,
+        out_specs=(pl.BlockSpec(memory_space=vmem),) * 2,
         scratch_shapes=[
             pltpu.SMEM(blocks.shape[2:], jnp.int32),
             vmem((cap, block, block), f32),
@@ -358,14 +366,13 @@
             vmem((ITERS, n_smp, w_rows, cap * block), f32),
             vmem((rank, cap * block), f32),
             vmem((rank, cap * block), f32),
-            vmem(h_factor.shape, f32),
-            vmem(w_factor.shape, f32),
-            vmem((3 * rank, max(texels, samples)), half),
+            vmem((2 * cap * rank, max(texels, samples)), half),
+            vmem((cap * rank, max(texels, samples)), half),
             dma((phases, n_tex - 1)),
             dma((phases, n_tex - 1)),
             dma((phases, n_smp - 1)),
             dma((phases, n_smp - 1)),
-            dma((8,)),
+            dma((6,)),
         ],
         compiler_params=pltpu.CompilerParams(
             collective_id=0, has_side_effects=True, vmem_limit_bytes=60 * 2**20

time: 50.1 us -> 48.1 us (0.960)
  Pallas kernels: 47.3 us -> 46 us
  local copies, waits for them, and re-layouts: 2.04 us -> 1.25 us
    pallas_call x1, Pallas kernels: 47.3 us -> 46 us  [per_device(): pl.pallas_call(functools.partial(kernel, (n_tex, n_smp)), out_shape=(pltp...]
    unnamed x4 -> x2, local copies, waits for them, and re-layouts: 2.04 us -> 1.25 us
where the time goes in v4:
time: 48.1 us; the launch traced here: 47.9 us
  Pallas kernels  46 us (96%)
  local copies, waits for them, and re-layouts  1.25 us (3%)
  between operations  0.64 us (1%)
    pallas_call x1, Pallas kernels, per_device(): pl.pallas_call(functools.partial(kernel, (n_tex, n_smp)), out_shape=(pltp...  46 us
    unnamed x2, local copies, waits for them, and re-layouts  1.25 us

profile of v4, /device:TPU:0, one launch (start us, length us, event | category | flops | bytes accessed | tf_op | source)
XLA Modules:
  0.0 47.9 jit_solution(5151849888433858334)
XLA Ops:
  0.6 46.0 %shard_map.59 = (f32[8,1024]{1,0:T(8,128)S(1)}, f32[16,1024]{1,0:T(8,128)S(1)}) custom-call(s32[2,2]{1,0:T(2,128)} %bitcast.3, f32[2,256,256]{2,1,0:T(8,128)} %bitcast.2, f32[8,1024]{1,0:T(8,128)} %w_in.1, f32[16,1024]{1,0:T(8,128)} %h_in.1), custom_call_target="tpu_custom_call" | custom-call | tf_op jit(solution)/shard_map/pallas_call | solution.py:333
  46.7 0.6 %copy.8 = f32[8,1024]{1,0:T(8,128)} copy(f32[8,1024]{1,0:T(8,128)S(1)} %get-tuple-element.2) | data formatting | bytes 65536
  47.3 0.6 %copy.9 = f32[16,1024]{1,0:T(8,128)} copy(f32[16,1024]{1,0:T(8,128)S(1)} %get-tuple-element.3) | data formatting | bytes 131072

commit v5 on v4

--- a/solution.py
+++ b/solution.py
@@ -142,6 +142,10 @@
     notes = scatter("smp", 1, lambda to: note, smp_note.at[me_s])
     notes += scatter("tex", 1, lambda to: note, tex_note.at[me_t])
 
+    fetch[3].wait()
+    for j in range(cap):
+        high[j], low[j] = halves(values[j])
+        turned_high[j], turned_low[j] = halves(values[j].T)
     h_come = gather_forward("tex", 0, h_buf.at[0], h_come)
     w_come = gather_forward("smp", 0, w_buf.at[0], w_come)
     arrive(notes)
@@ -151,10 +155,6 @@
     ]
     for copy in copies:
         copy.start()
-    fetch[3].wait()
-    for j in range(cap):
-        high[j], low[j] = halves(values[j])
-        turned_high[j], turned_low[j] = halves(values[j].T)
     arrive(w_come)
     get_rows(w_full, w_buf.at[0])
 

time: 48.1 us -> 48.1 us (level)
  no operation moved by 1% of the time
where the time goes in v5:
time: 48.1 us; the launch traced here: 47.9 us
  Pallas kernels  46 us (96%)
  local copies, waits for them, and re-layouts  1.25 us (3%)
  between operations  0.64 us (1%)
    pallas_call x1, Pallas kernels, per_device(): pl.pallas_call(functools.partial(kernel, (n_tex, n_smp)), out_shape=(pltp...  46 us
    unnamed x2, local copies, waits for them, and re-layouts  1.25 us

profile of v5, /device:TPU:0, one launch (start us, length us, event | category | flops | bytes accessed | tf_op | source)
XLA Modules:
  0.0 47.9 jit_solution(5405342090183217192)
XLA Ops:
  0.6 46.0 %shard_map.59 = (f32[8,1024]{1,0:T(8,128)S(1)}, f32[16,1024]{1,0:T(8,128)S(1)}) custom-call(s32[2,2]{1,0:T(2,128)} %bitcast.3, f32[2,256,256]{2,1,0:T(8,128)} %bitcast.2, f32[8,1024]{1,0:T(8,128)} %w_in.1, f32[16,1024]{1,0:T(8,128)} %h_in.1), custom_call_target="tpu_custom_call" | custom-call | tf_op jit(solution)/shard_map/pallas_call | solution.py:333
  46.7 0.6 %copy.8 = f32[8,1024]{1,0:T(8,128)} copy(f32[8,1024]{1,0:T(8,128)S(1)} %get-tuple-element.2) | data formatting | bytes 65536
  47.3 0.6 %copy.9 = f32[16,1024]{1,0:T(8,128)} copy(f32[16,1024]{1,0:T(8,128)S(1)} %get-tuple-element.3) | data formatting | bytes 131072
